TPU v7x, 128 devices: a whole 4x4x4 slice. The times are simulated.
128 devices in a mesh: ctx: 16 (over x_lo, y, core), fsdp: 8 (over z, x_hi).
Axes of the slice: x: 4 (x_hi: 2, x_lo: 2; x = x_hi * 2 + x_lo), y: 4, z: 4, core: 2. Of those that a mesh axis runs over, the one named last changes fastest.
Arguments:
- query_rows: bfloat16 [16384, 2048], P('ctx', 'fsdp'), may hold values from -270 to 270
- key_rows: bfloat16 [16384, 1024], P('ctx', 'fsdp'), may hold values from -6 to 6
- value_rows: bfloat16 [16384, 1024], P('ctx', 'fsdp'), may hold values from -6 to 6
- doc_ids: int32 [16384], P('ctx'), may hold values from 0 to 3, never falling along the last dimension, each value on 1 to 6144 neighbouring positions
- out_weight: bfloat16 [2048, 4608], P('fsdp', 'ctx'), may hold values from -0.125 to 0.125
- out_grad: bfloat16 [16384, 4608], P('ctx'), may hold values from -6 to 6
Outputs:
- layer_out: bfloat16 [16384, 4608], P('ctx', 'fsdp')
- query_grad: bfloat16 [16384, 2048], P('ctx', 'fsdp')
- key_grad: bfloat16 [16384, 1024], P('ctx', 'fsdp')
- value_grad: bfloat16 [16384, 1024], P('ctx', 'fsdp')
- weight_grad: float32 [2048, 4608], P('fsdp', 'ctx')
Inputs may be any that keep to these rules, and one draw needn't show every extreme that they name: `doc_ids`: never falls along the sequence; each document has 1 to 6144 tokens and one has exactly 6144.
All inputs are finite; a program needn't handle non-finite values.
Results may differ from a plain program's by a relative error of at most 0.035.
Values may be sent and summed in bfloat16 or wider, within the bound.
No kernel may reach another device: no remote copies, remote signals or barrier semaphores. Data moves between devices by JAX's collectives and lax.ppermute only.
A program may use at most 256 MiB of HBM per device.

v0:
```python
import functools
import math

import jax
import jax.numpy as jnp
from jax import lax
from jax.experimental import pallas as pl
from jax.experimental.pallas import tpu as pltpu
from jax.sharding import Mesh, PartitionSpec as P

HEAD_DIM = 128
WINDOW = 4096
N_DOCS = 4
SCALE = 1.0 / 12.0
SCALE2 = math.log2(math.e) / 12.0
NEG = -1e30
FAR = 1 << 30
F32 = jnp.float32
BF16 = jnp.bfloat16
NT = (((1,), (1,)), ((), ()))
NN = (((1,), (0,)), ((), ()))

CTX = ("xl", "y", "core")
FSDP = ("z", "xh")


def first_seen(meta, i):
    low = i + 1
    for d in range(N_DOCS):
        low = jnp.maximum(low, jnp.where(i >= meta[d], meta[N_DOCS + d], 0))
    return low


def tile_bounds(meta, q0, bq, bk, win):
    start = first_seen(meta, q0) // bk
    end = (win + q0 + bq - 1) // bk + 1
    b = (win + q0 + 1) // bk
    a = (first_seen(meta, q0 + bq - 1) + bk - 1) // bk
    a = jnp.clip(a, start, end)
    b = jnp.clip(b, a, end)
    return start, a, b, end


def heads_of(ref, q0, bq):
    return jnp.concatenate(
        [ref[q0 : q0 + bq, 0:HEAD_DIM], ref[q0 : q0 + bq, HEAD_DIM : 2 * HEAD_DIM]], 0
    )


def masked_tile(meta, tile, q0, r, win, bq, bk):
    i = q0 + lax.broadcasted_iota(jnp.int32, (1, bq), 1)
    low = first_seen(meta, i) - r
    high = win + i - r
    row = lax.broadcasted_iota(jnp.int32, (bk, bq), 0)
    seen = (row >= low) & (row <= high)
    return jnp.concatenate(
        [jnp.where(seen, tile[:, :bq], NEG), jnp.where(seen, tile[:, bq:], NEG)], 1
    )


def forward_kernel(meta, q_ref, kv_ref, o_ref, lse_ref, m_ref, acc_ref, *, bq, bk):
    tok = q_ref.shape[0]
    win = kv_ref.shape[0] - tok
    for q0 in range(0, tok, bq):
        q2 = heads_of(q_ref, q0, bq)
        m_ref[...] = jnp.full(m_ref.shape, NEG, F32)
        acc_ref[...] = jnp.zeros(acc_ref.shape, F32)
        start, a, b, end = tile_bounds(meta, q0, bq, bk, win)

        def tile(j, masked):
            r = pl.multiple_of(j * bk, bk)
            k = kv_ref[pl.ds(r, bk), 0:HEAD_DIM]
            v = kv_ref[pl.ds(r, bk), HEAD_DIM : 2 * HEAD_DIM]
            s = lax.dot_general(k, q2, NT, preferred_element_type=F32)
            if masked:
                s = masked_tile(meta, s, q0, r, win, bq, bk)
            m_old = m_ref[0:1, :]
            m_new = jnp.maximum(m_old, jnp.max(s, axis=0, keepdims=True))
            p = jnp.exp2((s - m_new) * SCALE2)
            shrink = jnp.exp2((m_old - m_new) * SCALE2)
            v_ones = jnp.concatenate([v.T, jnp.ones((16, bk), BF16)], 0)
            acc_ref[...] = acc_ref[...] * shrink + lax.dot_general(
                v_ones, p.astype(BF16), NN, preferred_element_type=F32
            )
            m_ref[...] = jnp.broadcast_to(m_new, m_ref.shape)

        def down(high, low, masked):
            def step(t, carry):
                tile(high - 1 - t, masked)
                return carry

            lax.fori_loop(0, high - low, step, 0)

        down(end, b, True)
        down(b, a, False)
        down(a, start, True)
        total = acc_ref[HEAD_DIM : HEAD_DIM + 1, :]
        o = (acc_ref[0:HEAD_DIM, :] / total).T
        o_ref[q0 : q0 + bq, 0:HEAD_DIM] = o[:bq].astype(BF16)
        o_ref[q0 : q0 + bq, HEAD_DIM:] = o[bq:].astype(BF16)
        lse = m_ref[...] * SCALE2 + jnp.log2(acc_ref[HEAD_DIM : HEAD_DIM + 8, :])
        lse_ref[0:8, q0 : q0 + bq] = lse[:, :bq]
        lse_ref[8:16, q0 : q0 + bq] = lse[:, bq:]


def forward(meta, q, kv, bq=512, bk=512):
    tok = q.shape[0]
    vmem = pl.BlockSpec(memory_space=pltpu.VMEM)
    return pl.pallas_call(
        functools.partial(forward_kernel, bq=bq, bk=bk),
        out_shape=(
            jax.ShapeDtypeStruct((tok, 2 * HEAD_DIM), BF16),
            jax.ShapeDtypeStruct((16, tok), F32),
        ),
        in_specs=[pl.BlockSpec(memory_space=pltpu.SMEM), vmem, vmem],
        out_specs=(vmem, vmem),
        scratch_shapes=[
            pltpu.VMEM((8, 2 * bq), F32),
            pltpu.VMEM((HEAD_DIM + 16, 2 * bq), F32),
        ],
        compiler_params=pltpu.CompilerParams(vmem_limit_bytes=40 * 2**20),
        cost_estimate=pl.CostEstimate(
            flops=20_000_000_000, bytes_accessed=4_000_000, transcendentals=9_000_000
        ),
        name="attn_forward",
    )(meta, q, kv)


def backward_kernel(
    meta, q_ref, kv_ref, o_ref, do_ref, lse_ref, dq_ref, dkv_ref, own_ref, dqt, dk, dv, *, bq, bk
):
    tok = q_ref.shape[0]
    win = kv_ref.shape[0] - tok
    dk[...] = jnp.zeros(dk.shape, F32)
    dv[...] = jnp.zeros(dv.shape, F32)
    for q0 in range(0, tok, bq):
        q2 = heads_of(q_ref, q0, bq)
        do2 = heads_of(do_ref, q0, bq)
        o2 = heads_of(o_ref, q0, bq)
        delta = jnp.sum((do2.astype(F32) * o2.astype(F32)).T, axis=0, keepdims=True)
        lse = jnp.concatenate([lse_ref[0:1, q0 : q0 + bq], lse_ref[8:9, q0 : q0 + bq]], 1)
        dqt[...] = jnp.zeros(dqt.shape, F32)
        start, a, b, end = tile_bounds(meta, q0, bq, bk, win)

        def tile(j, masked):
            r = pl.multiple_of(j * bk, bk)
            k = kv_ref[pl.ds(r, bk), 0:HEAD_DIM]
            v = kv_ref[pl.ds(r, bk), HEAD_DIM : 2 * HEAD_DIM]
            t = lax.dot_general(k, q2, NT, preferred_element_type=F32) * SCALE2 - lse
            if masked:
                t = masked_tile(meta, t, q0, r, win, bq, bk)
            p = jnp.exp2(t)
            dp = lax.dot_general(v, do2, NT, preferred_element_type=F32)
            ds = (p * (dp - delta)).astype(BF16)
            dv[pl.ds(r, bk), :] += lax.dot_general(
                p.astype(BF16), do2, NN, preferred_element_type=F32
            )
            dk[pl.ds(r, bk), :] += lax.dot_general(ds, q2, NN, preferred_element_type=F32)
            dqt[...] += lax.dot_general(k.T, ds, NN, preferred_element_type=F32)

        def up(low, high, masked):
            def step(t, carry):
                tile(t, masked)
                return carry

            lax.fori_loop(low, high, step, 0)

        up(start, a, True)
        up(a, b, False)
        up(b, end, True)
        dq = (dqt[...] * SCALE).T
        dq_ref[q0 : q0 + bq, 0:HEAD_DIM] = dq[:bq].astype(BF16)
        dq_ref[q0 : q0 + bq, HEAD_DIM:] = dq[bq:].astype(BF16)
    dkv_ref[:, 0:HEAD_DIM] = (dk[0:win] * SCALE).astype(BF16)
    dkv_ref[:, HEAD_DIM:] = dv[0:win].astype(BF16)
    own_ref[:, 0:HEAD_DIM] = dk[win:] * SCALE
    own_ref[:, HEAD_DIM:] = dv[win:]


def backward(meta, q, kv, o, do, lse, bq=512, bk=512):
    tok = q.shape[0]
    win = kv.shape[0] - tok
    vmem = pl.BlockSpec(memory_space=pltpu.VMEM)
    return pl.pallas_call(
        functools.partial(backward_kernel, bq=bq, bk=bk),
        out_shape=(
            jax.ShapeDtypeStruct((tok, 2 * HEAD_DIM), BF16),
            jax.ShapeDtypeStruct((win, 2 * HEAD_DIM), BF16),
            jax.ShapeDtypeStruct((tok, 2 * HEAD_DIM), F32),
        ),
        in_specs=[pl.BlockSpec(memory_space=pltpu.SMEM)] + [vmem] * 5,
        out_specs=(vmem, vmem, vmem),
        scratch_shapes=[
            pltpu.VMEM((HEAD_DIM, 2 * bq), F32),
            pltpu.VMEM((tok + win, HEAD_DIM), F32),
            pltpu.VMEM((tok + win, HEAD_DIM), F32),
        ],
        compiler_params=pltpu.CompilerParams(vmem_limit_bytes=40 * 2**20),
        cost_estimate=pl.CostEstimate(
            flops=30_000_000_000, bytes_accessed=8_000_000, transcendentals=9_000_000
        ),
        name="attn_backward",
    )(meta, q, kv, o, do, lse)


def ctx_shift(value, steps):
    count = lax.axis_size(CTX)
    leading, last = max(0, -steps), min(count, count - steps)
    return lax.ppermute(value, CTX, [(s, s + steps) for s in range(leading, last)])


def swap(value, axis):
    return lax.ppermute(value, axis, [(0, 1), (1, 0)])


def z_shift(value, steps):
    count = lax.axis_size("z")
    return lax.ppermute(value, "z", [(s, (s + steps) % count) for s in range(count)])


def body(query_rows, key_rows, value_rows, doc_ids, out_weight, out_grad):
    tok = query_rows.shape[0]
    core = lax.axis_index("core")
    z = lax.axis_index("z")
    xh = lax.axis_index("xh")
    n_z = lax.axis_size("z")

    docs = lax.iota(jnp.int32, N_DOCS)
    count = jnp.sum((doc_ids[None, :] == docs[:, None]).astype(jnp.int32), axis=1)
    info = jnp.stack([count // 32, count % 32]).astype(BF16)
    info = jnp.pad(info, ((0, 14), (0, 2 * HEAD_DIM - N_DOCS)))
    kv = jnp.concatenate([key_rows, value_rows], 1)
    load = jnp.concatenate([kv, info], 0)
    back2 = ctx_shift(load, 2)
    back4 = ctx_shift(load, 4)
    back1 = swap(jnp.where(core == 0, load, back2), "core")
    back3 = swap(jnp.where(core == 0, back2, back4), "core")
    blocks = [back4, back3, back2, back1]
    window = jnp.concatenate([b[:tok] for b in blocks] + [kv], 0)
    infos = sum(b[tok : tok + 2, :N_DOCS].astype(F32) for b in blocks)
    before = (infos[0] * 32 + infos[1]).astype(jnp.int32)
    local_start = jnp.cumsum(count) - count
    present = count > 0
    meta = jnp.concatenate(
        [
            jnp.where(present, local_start, FAR),
            jnp.where(present, WINDOW + local_start - before, 0),
        ]
    )

    weight_t = lax.all_gather(out_weight.T, CTX, axis=0, tiled=True)
    attn, lse = forward(meta, query_rows, window)
    d_attn = jnp.dot(out_grad, weight_t, preferred_element_type=F32).astype(BF16)

    weight_z = weight_t.reshape(n_z, -1, weight_t.shape[1])

    def weight_for(steps):
        return lax.dynamic_index_in_dim(weight_z, (z + steps) % n_z, 0, keepdims=False)

    weights = [weight_for(0)] + [z_shift(weight_for(s), s) for s in range(1, n_z)]
    attns = [attn] + [z_shift(attn, s) for s in range(1, n_z)]
    cols = weights[0].shape[0] // 2

    def out_part(half):
        total = None
        for a, w in zip(attns, weights):
            w = lax.dynamic_slice_in_dim(w, half * cols, cols, 0)
            term = lax.dot_general(a, w, NT, preferred_element_type=F32)
            total = term if total is None else total + term
        return total

    out_other = swap(out_part(1 - xh).astype(BF16), "xh")

    d_weight = lax.dot_general(
        out_grad, attn, (((0,), (0,)), ((), ())), preferred_element_type=F32
    ).astype(BF16)
    weight_grad = lax.psum_scatter(d_weight, CTX, scatter_dimension=0, tiled=True).astype(F32).T

    query_grad, d_window, own = backward(meta, query_rows, window, attn, d_attn, lse)
    part4, part3, part2, part1 = (d_window[i * tok : (i + 1) * tok] for i in range(4))
    other3 = swap(part3, "core").astype(F32)
    other1 = swap(part1, "core").astype(F32)
    even = core == 0
    sum4 = (part4.astype(F32) + jnp.where(even, 0.0, other3)).astype(BF16)
    sum2 = (part2.astype(F32) + jnp.where(even, other3, other1)).astype(BF16)
    own = own + jnp.where(even, other1, 0.0)
    own = own + ctx_shift(sum4, -4).astype(F32) + ctx_shift(sum2, -2).astype(F32)
    own = own.astype(BF16)

    layer_out = (out_part(xh) + out_other.astype(F32)).astype(BF16)
    return layer_out, query_grad, own[:, :HEAD_DIM], own[:, HEAD_DIM:], weight_grad


def solution(mesh):
    fine = Mesh(mesh.devices.reshape(2, 4, 2, 4, 2), CTX + FSDP)
    in_specs = (
        P(CTX, FSDP),
        P(CTX, FSDP),
        P(CTX, FSDP),
        P(CTX),
        P(FSDP, CTX),
        P(CTX, None),
    )
    out_specs = (
        P(CTX, FSDP),
        P(CTX, FSDP),
        P(CTX, FSDP),
        P(CTX, FSDP),
        P(FSDP, CTX),
    )
    return jax.shard_map(body, mesh=fine, in_specs=in_specs, out_specs=out_specs, check_vma=False)
```

profile of v0, /device:TPU:52, one launch (start us, length us, event | category | flops | bytes accessed | tf_op | source)
XLA Modules:
  0.0 217.4 jit_solution(14239760399341038643)
XLA Ops:
  7.2 0.8 convert_reduce_fusion
  8.1 1.1 pad_maximum_fusion
  9.1 2.9 %collective-permute-start = (bf16[1040,256]{1,0:T(8,128)(2,1)S(1)}, bf16[1040,256]{1,0:T(8,128)(2,1)S(1)}, u32[]{:S(2)}, u32[]{:S(2)}) collective-permute-start(bf16[1040,256]{1,0:T(8,128)(2,1)S(1)} %pad_maximum_fusion), channel_id=1, source_target_pairs={{0,32},{8,40},{16,48},{24,56},{32,64},{40,72},{48,80},{56,88},{64,... | collective-permute-start | bytes 1597448 | tf_op jit(solution)/shard_map/ppermute | solution.py:209
  12.0 4.1 %collective-permute-start.1 = (bf16[1040,256]{1,0:T(8,128)(2,1)S(1)}, bf16[1040,256]{1,0:T(8,128)(2,1)S(1)}, u32[]{:S(2)}, u32[]{:S(2)}) collective-permute-start(bf16[1040,256]{1,0:T(8,128)(2,1)S(1)} %pad_maximum_fusion), channel_id=1, source_target_pairs={{0,16},{8,24},{16,32},{24,40},{32,48},{40,56},{48,64},{56,72},{64,... | collective-permute-start | bytes 1597448 | tf_op jit(solution)/shard_map/ppermute | solution.py:209
  16.1 11.4 %collective-permute-done = bf16[1040,256]{1,0:T(8,128)(2,1)S(1)} collective-permute-done((bf16[1040,256]{1,0:T(8,128)(2,1)S(1)}, bf16[1040,256]{1,0:T(8,128)(2,1)S(1)}, u32[]{:S(2)}, u32[]{:S(2)}) %collective-permute-start) | collective-permute-done | bytes 532512 | tf_op jit(solution)/shard_map/ppermute | solution.py:209
  27.6 10.2 %collective-permute-done.1 = bf16[1040,256]{1,0:T(8,128)(2,1)S(1)} collective-permute-done((bf16[1040,256]{1,0:T(8,128)(2,1)S(1)}, bf16[1040,256]{1,0:T(8,128)(2,1)S(1)}, u32[]{:S(2)}, u32[]{:S(2)}) %collective-permute-start.1) | collective-permute-done | bytes 532512 | tf_op jit(solution)/shard_map/ppermute | solution.py:209
  37.8 0.8 copy-done.5
  38.6 2.3 %broadcast_select_fusion.1 = (bf16[1040,256]{1,0:T(8,128)(2,1)}, bf16[1040,256]{1,0:T(8,128)(2,1)}) fusion(bf16[1040,256]{1,0:T(8,128)(2,1)S(1)} %collective-permute-done.1, bf16[1040,256]{1,0:T(8,128)(2,1)S(1)} %collective-permute-done, pred[]{:T(512)S(6)} %eq.28, bf16[16,256]{1,0:T(8,128)(2,1)S(1)} %fusion.34, bf16[1024,128]{1,0:T(8,128)(2,1)} %param.8, ...), kind=kLoop, calls=%fused_computation.21 | loop fusion | flops 2129920 | bytes 2662401 | tf_op jit(solution)/shard_map/jit(_where)/select_n | solution.py:237
  40.9 0.5 collective-permute-start.3
  41.7 1.1 slice_dynamic-update-slice_fusion.3
  42.9 0.3 collective-permute-done.2
  43.2 0.8 collective-permute-done.3
  43.9 0.7 convert_add_fusion
  44.7 1.1 slice_dynamic-update-slice_fusion.2
  45.8 1.1 slice_dynamic-update-slice_fusion
  47.1 21.2 %attn_forward.1 = (bf16[1024,256]{1,0:T(8,128)(2,1)S(1)}, f32[16,1024]{1,0:T(8,128)S(1)}) custom-call(s32[8]{0:T(128)S(1)} %pad_add_fusion.meta, bf16[1024,256]{1,0:T(8,128)(2,1)S(1)} %copy-done, bf16[5120,256]{1,0:T(8,128)(2,1)S(1)} %constant_dynamic-update-slice_fusion.1.kv_ref), custom_call_target="tpu_custom_call" | custom-call | flops 20000000000 | bytes 4000000 | tf_op jit(solution)/shard_map/attn_forward/pallas_call | solution.py:109
  68.4 2.2 collective-permute-start.4
  70.5 3.9 %fusion = bf16[4608,256]{0,1:T(8,128)(2,1)} fusion(bf16[1024,256]{1,0:T(8,128)(2,1)S(1)} %get-tuple-element.10.o_ref, bf16[1024,4608]{1,0:T(8,128)(2,1)S(1)} %bitcast.60), kind=kOutput, calls=%fused_computation.1 | convolution fusion | flops 2417098752 | bytes 12320768 | tf_op jit(solution)/shard_map/dot_general | solution.py:274
  74.4 4.3 %copy.14 = bf16[4608,256]{1,0:T(8,128)(2,1)} copy(bf16[4608,256]{0,1:T(8,128)(2,1)} %fusion) | data formatting | bytes 4718592
  78.8 7.0 %convolution_convert_fusion.1.do_ref = bf16[1024,256]{1,0:T(8,128)(2,1)S(1)} fusion(bf16[1024,4608]{1,0:T(8,128)(2,1)} %param.11, bf16[4608,256]{1,0:T(8,128)(2,1)} %all-gather.2.cloned.1.call-done), kind=kOutput, calls=%fused_computation.7 | convolution fusion | flops 2416181248 | bytes 12320768 | tf_op jit(solution)/shard_map/dot_general | solution.py:253
  85.8 29.4 %attn_backward.1 = (bf16[1024,256]{1,0:T(8,128)(2,1)}, bf16[4096,256]{1,0:T(8,128)(2,1)S(1)}, f32[1024,256]{1,0:T(8,128)S(1)}) custom-call(s32[8]{0:T(128)S(1)} %pad_add_fusion.meta, bf16[1024,256]{1,0:T(8,128)(2,1)S(1)} %copy-done.1, bf16[5120,256]{1,0:T(8,128)(2,1)S(1)} %constant_dynamic-update-slice_fusion.1.kv_ref, ...), custom_call_target="tpu_custom_call" | custom-call | flops 30000001024 | bytes 8000000 | tf_op jit(solution)/shard_map/attn_backward/pallas_call | solution.py:184
  115.3 4.4 %collective-permute-start.11 = (bf16[1024,256]{1,0:T(8,128)(2,1)S(1)}, bf16[1024,256]{1,0:T(8,128)(2,1)S(1)}, u32[]{:S(2)}, u32[]{:S(2)}) collective-permute-start(bf16[1024,256]{1,0:T(8,128)(2,1)S(1)} %get-tuple-element.36), channel_id=1, source_target_pairs={{0,8},{8,0},{1,9},{9,1},{2,10},{10,2},{3,11},{11,3},{4,12},{12,4},... | collective-permute-start | bytes 1572872 | tf_op jit(solution)/shard_map/ppermute | solution.py:213
  119.9 1.7 collective-permute-start.5
  121.6 0.6 collective-permute-start.7
  122.2 0.5 fusion.9
  122.7 0.5 fusion.11
  123.2 3.1 %collective-permute-start.6 = (bf16[1024,256]{1,0:T(8,128)(2,1)S(1)}, bf16[1024,256]{1,0:T(8,128)(2,1)S(1)}, u32[]{:S(2)}, u32[]{:S(2)}) collective-permute-start(bf16[1024,256]{1,0:T(8,128)(2,1)S(1)} %get-tuple-element.10.o_ref), channel_id=1, source_target_pairs={{0,4},{2,6},{4,0},{6,2},{1,5},{3,7},{5,1},{7,3},{8,12},{10,14},{12... | collective-permute-start | bytes 1572872 | tf_op jit(solution)/shard_map/ppermute | solution.py:218
  126.3 0.4 collective-permute-start.8
  126.7 0.3 fusion.6
  127.0 1.4 collective-permute-start.9
  128.4 7.7 %collective-permute-done.5 = bf16[1152,256]{1,0:T(8,128)(2,1)S(1)} collective-permute-done((bf16[1152,256]{1,0:T(8,128)(2,1)S(1)}, bf16[1152,256]{1,0:T(8,128)(2,1)S(1)}, u32[]{:S(2)}, u32[]{:S(2)}) %collective-permute-start.5) | collective-permute-done | bytes 589856 | tf_op jit(solution)/shard_map/ppermute | solution.py:218
  136.1 1.9 collective-permute-start.13
  138.1 1.6 fusion.19
  139.6 11.0 %collective-permute-done.6 = bf16[1024,256]{1,0:T(8,128)(2,1)S(1)} collective-permute-done((bf16[1024,256]{1,0:T(8,128)(2,1)S(1)}, bf16[1024,256]{1,0:T(8,128)(2,1)S(1)}, u32[]{:S(2)}, u32[]{:S(2)}) %collective-permute-start.6) | collective-permute-done | bytes 524320 | tf_op jit(solution)/shard_map/ppermute | solution.py:218
  150.6 1.9 collective-permute-start.14
  152.5 0.5 fusion.17
  153.0 8.1 %collective-permute-done.8 = bf16[1024,256]{1,0:T(8,128)(2,1)S(1)} collective-permute-done((bf16[1024,256]{1,0:T(8,128)(2,1)S(1)}, bf16[1024,256]{1,0:T(8,128)(2,1)S(1)}, u32[]{:S(2)}, u32[]{:S(2)}) %collective-permute-start.8) | collective-permute-done | bytes 524320 | tf_op jit(solution)/shard_map/ppermute | solution.py:218
  161.1 12.5 %collective-permute-done.9 = bf16[1152,256]{1,0:T(8,128)(2,1)S(1)} collective-permute-done((bf16[1152,256]{1,0:T(8,128)(2,1)S(1)}, bf16[1152,256]{1,0:T(8,128)(2,1)S(1)}, u32[]{:S(2)}, u32[]{:S(2)}) %collective-permute-start.9) | collective-permute-done | bytes 589856 | tf_op jit(solution)/shard_map/ppermute | solution.py:218
  173.6 1.6 add_convert_fusion.1
  175.2 0.5 collective-permute-start.10
  175.7 1.9 fusion.22
  177.6 2.0 fusion.24
  179.6 3.0 %fusion.26 = f32[1024,576]{0,1:T(8,128)} fusion(bf16[1024,256]{1,0:T(8,128)(2,1)} %collective-permute-done.4, bf16[1152,256]{1,0:T(8,128)(2,1)S(1)} %collective-permute-done.5, s32[]{:T(128)S(6)} %select_n.124), kind=kOutput, calls=%fused_computation.42 | convolution fusion | flops 301989888 | bytes 3178500 | tf_op jit(solution)/shard_map/dot_general | solution.py:268
  182.9 0.8 fusion.46
  183.7 1.1 copy.15
  184.8 0.9 copy.13
  185.7 19.2 %collective-permute-done.10 = bf16[1024,576]{0,1:T(8,128)(2,1)} collective-permute-done((bf16[1024,576]{0,1:T(8,128)(2,1)}, bf16[1024,576]{0,1:T(8,128)(2,1)}, u32[]{:S(2)}, u32[]{:S(2)}) %collective-permute-start.10) | collective-permute-done | bytes 1179680 | tf_op jit(solution)/shard_map/ppermute | solution.py:213
  204.9 5.6 %add_convert_fusion = bf16[1024,576]{0,1:T(8,128)(2,1)} fusion(bf16[1024,576]{0,1:T(8,128)(2,1)} %collective-permute-done.10, f32[1024,576]{0,1:T(8,128)} %fusion.22, f32[1024,576]{0,1:T(8,128)} %fusion.24, f32[1024,576]{0,1:T(8,128)S(1)} %fusion.11, f32[1024,576]{0,1:T(8,128)} %fusion.26), kind=kLoop, calls=%fused_computation.2 | loop fusion | flops 3538944 | bytes 11796480 | tf_op jit(solution)/shard_map/convert_element_type | solution.py:290
  (48 shorter events, 1.2 us)
Async XLA Ops:
  7.2 71.6 %all-gather.2.cloned.1.call-start = ((), (), s32[]{:S(2)}) async-start(), calls=%async_computation.1 | async-start | bytes 2506752 | tf_op jit(solution)/shard_map/all_gather | solution.py:251
  9.1 18.4 %collective-permute-start = (bf16[1040,256]{1,0:T(8,128)(2,1)S(1)}, bf16[1040,256]{1,0:T(8,128)(2,1)S(1)}, u32[]{:S(2)}, u32[]{:S(2)}) collective-permute-start(bf16[1040,256]{1,0:T(8,128)(2,1)S(1)} %pad_maximum_fusion), channel_id=1, source_target_pairs={{0,32},{8,40},{16,48},{24,56},{32,64},{40,72},{48,80},{56,88},{64,... | collective-permute-start | bytes 1597448 | tf_op jit(solution)/shard_map/ppermute | solution.py:209
  12.0 25.8 %collective-permute-start.1 = (bf16[1040,256]{1,0:T(8,128)(2,1)S(1)}, bf16[1040,256]{1,0:T(8,128)(2,1)S(1)}, u32[]{:S(2)}, u32[]{:S(2)}) collective-permute-start(bf16[1040,256]{1,0:T(8,128)(2,1)S(1)} %pad_maximum_fusion), channel_id=1, source_target_pairs={{0,16},{8,24},{16,32},{24,40},{32,48},{40,56},{48,64},{56,72},{64,... | collective-permute-start | bytes 1597448 | tf_op jit(solution)/shard_map/ppermute | solution.py:209
  27.6 14.1 %copy-start.7 = (bf16[1040,256]{1,0:T(8,128)(2,1)}, bf16[1040,256]{1,0:T(8,128)(2,1)S(1)}, u32[]{:S(2)}) copy-start(bf16[1040,256]{1,0:T(8,128)(2,1)S(1)} %collective-permute-done) | copy-start | bytes 1597444
  37.8 0.8 copy-start.5
  40.9 6.0 %copy-start.3 = (bf16[1024,128]{1,0:T(8,128)(2,1)S(1)}, bf16[1024,128]{1,0:T(8,128)(2,1)}, u32[]{:S(2)}) copy-start(bf16[1024,128]{1,0:T(8,128)(2,1)} %param.7) | copy-start | bytes 786436
  40.9 2.3 %collective-permute-start.2 = (bf16[1040,256]{1,0:T(8,128)(2,1)}, bf16[1040,256]{1,0:T(8,128)(2,1)}, u32[]{:S(2)}, u32[]{:S(2)}) collective-permute-start(bf16[1040,256]{1,0:T(8,128)(2,1)} %get-tuple-element.37), channel_id=1, source_target_pairs={{0,8},{8,0},{1,9},{9,1},{2,10},{10,2},{3,11},{11,3},{4,12},{12,4},... | collective-permute-start | bytes 1597448 | tf_op jit(solution)/shard_map/ppermute | solution.py:213
  40.9 3.0 %collective-permute-start.3 = (bf16[1040,256]{1,0:T(8,128)(2,1)}, bf16[1040,256]{1,0:T(8,128)(2,1)}, u32[]{:S(2)}, u32[]{:S(2)}) collective-permute-start(bf16[1040,256]{1,0:T(8,128)(2,1)} %get-tuple-element.38), channel_id=1, source_target_pairs={{0,8},{8,0},{1,9},{9,1},{2,10},{10,2},{3,11},{11,3},{4,12},{12,4},... | collective-permute-start | bytes 1597448 | tf_op jit(solution)/shard_map/ppermute | solution.py:213
  41.4 142.3 %reduce-scatter.4.cloned.1.call-start = ((), (), s32[]{:S(2)}) async-start(), calls=%async_computation.2 | async-start | bytes 2506752
  41.7 4.1 %copy-start.6 = (bf16[1040,256]{1,0:T(8,128)(2,1)S(1)}, bf16[1040,256]{1,0:T(8,128)(2,1)}, u32[]{:S(2)}) copy-start(bf16[1040,256]{1,0:T(8,128)(2,1)} %copy-done.5) | copy-start | bytes 1597444
  41.7 5.3 %copy-start.4 = (bf16[1024,128]{1,0:T(8,128)(2,1)S(1)}, bf16[1024,128]{1,0:T(8,128)(2,1)}, u32[]{:S(2)}) copy-start(bf16[1024,128]{1,0:T(8,128)(2,1)} %param.8) | copy-start | bytes 786436
  42.9 4.2 %copy-start = (bf16[1024,256]{1,0:T(8,128)(2,1)S(1)}, bf16[1024,256]{1,0:T(8,128)(2,1)}, u32[]{:S(2)}) copy-start(bf16[1024,256]{1,0:T(8,128)(2,1)} %q_ref.3) | copy-start | bytes 1572868
  47.0 23.5 %slice-start = ((s8[9437184]{0:T(1024)(128)(4,1)}), s8[4194304]{0:T(1024)(128)(4,1)S(1)}, s32[]{:S(2)}) async-start(s8[9437184]{0:T(1024)(128)(4,1)} %bitcast.59), calls=%async_computation.3 | async-start | bytes 8388608
  47.1 23.4 %slice-start.1 = ((s8[9437184]{0:T(1024)(128)(4,1)}), s8[4194304]{0:T(1024)(128)(4,1)S(1)}, s32[]{:S(2)}) async-start(s8[9437184]{0:T(1024)(128)(4,1)} %bitcast.59), calls=%async_computation.4 | async-start | bytes 8388608
  47.1 23.4 %slice-start.2 = ((s8[9437184]{0:T(1024)(128)(4,1)}), s8[1048576]{0:T(1024)(128)(4,1)S(1)}, s32[]{:S(2)}) async-start(s8[9437184]{0:T(1024)(128)(4,1)} %bitcast.59), calls=%async_computation.5 | async-start | bytes 2097152
  68.4 58.6 %collective-permute-start.4 = (bf16[1024,256]{1,0:T(8,128)(2,1)S(1)}, bf16[1024,256]{1,0:T(8,128)(2,1)}, u32[]{:S(2)}, u32[]{:S(2)}) collective-permute-start(bf16[1024,256]{1,0:T(8,128)(2,1)S(1)} %get-tuple-element.10.o_ref), channel_id=1, source_target_pairs={{0,2},{2,4},{4,6},{6,0},{1,3},{3,5},{5,7},{7,1},{8,10},{10,12},{12... | collective-permute-start | bytes 1572872 | tf_op jit(solution)/shard_map/ppermute | solution.py:218
  78.8 7.0 %copy-start.1 = (bf16[1024,256]{1,0:T(8,128)(2,1)S(1)}, bf16[1024,256]{1,0:T(8,128)(2,1)}, u32[]{:S(2)}) copy-start(bf16[1024,256]{1,0:T(8,128)(2,1)} %q_ref.3) | copy-start | bytes 1572868
  85.8 34.0 %copy-start.2 = (bf16[4608,256]{1,0:T(8,128)(2,1)S(1)}, bf16[4608,256]{1,0:T(8,128)(2,1)}, u32[]{:S(2)}) copy-start(bf16[4608,256]{1,0:T(8,128)(2,1)} %all-gather.2.cloned.1.call-done) | copy-start | bytes 7077892
  115.3 7.9 %collective-permute-start.11 = (bf16[1024,256]{1,0:T(8,128)(2,1)S(1)}, bf16[1024,256]{1,0:T(8,128)(2,1)S(1)}, u32[]{:S(2)}, u32[]{:S(2)}) collective-permute-start(bf16[1024,256]{1,0:T(8,128)(2,1)S(1)} %get-tuple-element.36), channel_id=1, source_target_pairs={{0,8},{8,0},{1,9},{9,1},{2,10},{10,2},{3,11},{11,3},{4,12},{12,4},... | collective-permute-start | bytes 1572872 | tf_op jit(solution)/shard_map/ppermute | solution.py:213
  119.7 6.6 %collective-permute-start.12 = (bf16[1024,256]{1,0:T(8,128)(2,1)S(1)}, bf16[1024,256]{1,0:T(8,128)(2,1)S(1)}, u32[]{:S(2)}, u32[]{:S(2)}) collective-permute-start(bf16[1024,256]{1,0:T(8,128)(2,1)S(1)} %get-tuple-element.35), channel_id=1, source_target_pairs={{0,8},{8,0},{1,9},{9,1},{2,10},{10,2},{3,11},{11,3},{4,12},{12,4},... | collective-permute-start | bytes 1572872 | tf_op jit(solution)/shard_map/ppermute | solution.py:213
  119.9 16.2 %collective-permute-start.5 = (bf16[1152,256]{1,0:T(8,128)(2,1)S(1)}, bf16[1152,256]{1,0:T(8,128)(2,1)S(1)}, u32[]{:S(2)}, u32[]{:S(2)}) collective-permute-start(bf16[1152,256]{1,0:T(8,128)(2,1)S(1)} %get-tuple-element.34), channel_id=1, source_target_pairs={{0,2},{2,4},{4,6},{6,0},{1,3},{3,5},{5,7},{7,1},{8,10},{10,12},{12... | collective-permute-start | bytes 1769480 | tf_op jit(solution)/shard_map/ppermute | solution.py:218
  121.6 30.9 %collective-permute-start.7 = (bf16[1152,256]{1,0:T(8,128)(2,1)S(1)}, bf16[1152,256]{1,0:T(8,128)(2,1)S(1)}, u32[]{:S(2)}, u32[]{:S(2)}) collective-permute-start(bf16[1152,256]{1,0:T(8,128)(2,1)S(1)} %get-tuple-element.33), channel_id=1, source_target_pairs={{0,4},{2,6},{4,0},{6,2},{1,5},{3,7},{5,1},{7,3},{8,12},{10,14},{12... | collective-permute-start | bytes 1769480 | tf_op jit(solution)/shard_map/ppermute | solution.py:218
  123.2 27.4 %collective-permute-start.6 = (bf16[1024,256]{1,0:T(8,128)(2,1)S(1)}, bf16[1024,256]{1,0:T(8,128)(2,1)S(1)}, u32[]{:S(2)}, u32[]{:S(2)}) collective-permute-start(bf16[1024,256]{1,0:T(8,128)(2,1)S(1)} %get-tuple-element.10.o_ref), channel_id=1, source_target_pairs={{0,4},{2,6},{4,0},{6,2},{1,5},{3,7},{5,1},{7,3},{8,12},{10,14},{12... | collective-permute-start | bytes 1572872 | tf_op jit(solution)/shard_map/ppermute | solution.py:218
  126.3 34.8 %collective-permute-start.8 = (bf16[1024,256]{1,0:T(8,128)(2,1)S(1)}, bf16[1024,256]{1,0:T(8,128)(2,1)S(1)}, u32[]{:S(2)}, u32[]{:S(2)}) collective-permute-start(bf16[1024,256]{1,0:T(8,128)(2,1)S(1)} %get-tuple-element.10.o_ref), channel_id=1, source_target_pairs={{0,6},{2,0},{4,2},{6,4},{1,7},{3,1},{5,3},{7,5},{8,14},{10,8},{12,... | collective-permute-start | bytes 1572872 | tf_op jit(solution)/shard_map/ppermute | solution.py:218
  127.0 46.6 %collective-permute-start.9 = (bf16[1152,256]{1,0:T(8,128)(2,1)S(1)}, bf16[1152,256]{1,0:T(8,128)(2,1)S(1)}, u32[]{:S(2)}, u32[]{:S(2)}) collective-permute-start(bf16[1152,256]{1,0:T(8,128)(2,1)S(1)} %get-tuple-element.32), channel_id=1, source_target_pairs={{0,6},{2,0},{4,2},{6,4},{1,7},{3,1},{5,3},{7,5},{8,14},{10,8},{12,... | collective-permute-start | bytes 1769480 | tf_op jit(solution)/shard_map/ppermute | solution.py:218
  136.1 46.5 %collective-permute-start.13 = (bf16[1024,256]{1,0:T(8,128)(2,1)S(1)}, bf16[1024,256]{1,0:T(8,128)(2,1)S(1)}, u32[]{:S(2)}, u32[]{:S(2)}) collective-permute-start(bf16[1024,256]{1,0:T(8,128)(2,1)S(1)} %get-tuple-element.30), channel_id=1, source_target_pairs={{32,0},{40,8},{48,16},{56,24},{64,32},{72,40},{80,48},{88,56},{96,... | collective-permute-start | bytes 1572872 | tf_op jit(solution)/shard_map/ppermute | solution.py:209
  150.6 32.1 %collective-permute-start.14 = (bf16[1024,256]{1,0:T(8,128)(2,1)S(1)}, bf16[1024,256]{1,0:T(8,128)(2,1)S(1)}, u32[]{:S(2)}, u32[]{:S(2)}) collective-permute-start(bf16[1024,256]{1,0:T(8,128)(2,1)S(1)} %get-tuple-element.31), channel_id=1, source_target_pairs={{16,0},{24,8},{32,16},{40,24},{48,32},{56,40},{64,48},{72,56},{80,... | collective-permute-start | bytes 1572872 | tf_op jit(solution)/shard_map/ppermute | solution.py:209
  175.2 29.7 %collective-permute-start.10 = (bf16[1024,576]{0,1:T(8,128)(2,1)}, bf16[1024,576]{0,1:T(8,128)(2,1)}, u32[]{:S(2)}, u32[]{:S(2)}) collective-permute-start(bf16[1024,576]{0,1:T(8,128)(2,1)} %add_convert_fusion.1), channel_id=1, source_target_pairs={{0,1},{1,0},{2,3},{3,2},{4,5},{5,4},{6,7},{7,6},{8,9},{9,8},{10,11... | collective-permute-start | bytes 3538952 | tf_op jit(solution)/shard_map/ppermute | solution.py:213
Sparse Core Ops, SparseCore 0:
  41.6 34.9 all-gather.1
  78.9 61.3 reduce-scatter.3
where the time goes:
time: 216 us; the launch traced here: 217 us
  waiting for transfers between devices  81.3 us (38%)
  Pallas kernels  50.6 us (23%)
  starting transfers between devices  25.7 us (12%)
  matrix products  22.5 us (10%)
  between operations  14.4 us (7%)
  local copies, waits for them, and re-layouts  11.5 us (5%)
  other arithmetic  11.4 us (5%)
    ppermute x6, waiting for transfers between devices, z_shift(): lax.ppermute(value, 'z', [(s, (s + steps) % count) for s in range(count)])  39.3 us
    pallas_call x1, Pallas kernels, backward(): pl.pallas_call(functools.partial(backward_kernel, bq=bq, bk=bk), out_shap...  29.4 us
    ppermute x4, waiting for transfers between devices, ctx_shift(): lax.ppermute(value, CTX, [(s, s + steps) for s in range(leading, last)])  21.7 us
    pallas_call x1, Pallas kernels, forward(): pl.pallas_call(functools.partial(forward_kernel, bq=bq, bk=bk), out_shape...  21.2 us
    ppermute x5, waiting for transfers between devices, swap(): return lax.ppermute(value, axis, [(0, 1), (1, 0)])  20.3 us
    dot_general x8, matrix products, out_part(): term = lax.dot_general(a, w, NT, preferred_element_type=F32)  11.6 us
    ppermute x4, starting transfers between devices, ctx_shift(): lax.ppermute(value, CTX, [(s, s + steps) for s in range(leading, last)])  10.8 us
    unnamed x30, local copies, waits for them, and re-layouts  10.5 us
  transfers between devices with their start and end apart: 17, of which 9 were waited for; matrix products, arithmetic and copies ran while one was open for 16% of the time, Pallas kernels for 23%

commit v1 on v0

v1 whole, which is shorter than its diff:
```python
import functools
import math

import jax
import jax.numpy as jnp
from jax import lax
from jax.experimental import pallas as pl
from jax.experimental.pallas import tpu as pltpu
from jax.sharding import Mesh, PartitionSpec as P

HEAD_DIM = 128
WINDOW = 4096
N_DOCS = 4
SCALE = 1.0 / 12.0
SCALE2 = math.log2(math.e) / 12.0
NEG = -1e30
FAR = 1 << 30
F32 = jnp.float32
BF16 = jnp.bfloat16
NT = (((1,), (1,)), ((), ()))
NN = (((1,), (0,)), ((), ()))

TOK = 1024
BQ = 512
BK = 512

CTX = ("xl", "y", "core")
FSDP = ("z", "xh")


def first_seen(meta, i):
    low = i + 1
    for d in range(N_DOCS):
        low = jnp.maximum(low, jnp.where(i >= meta[d], meta[N_DOCS + d], 0))
    return low


def heads_of(ref, q0):
    rows = pl.ds(q0, BQ)
    return jnp.concatenate([ref[rows, 0:HEAD_DIM], ref[rows, HEAD_DIM : 2 * HEAD_DIM]], 0)


def masked_tile(meta, tile, q0, place):
    i = q0 + lax.broadcasted_iota(jnp.int32, (1, BQ), 1)
    low = first_seen(meta, i) - place
    high = WINDOW + i - place
    row = lax.broadcasted_iota(jnp.int32, (BK, BQ), 0)
    seen = (row >= low) & (row <= high)
    return jnp.concatenate(
        [jnp.where(seen, tile[:, :BQ], NEG), jnp.where(seen, tile[:, BQ:], NEG)], 1
    )


def for_tiles(meta, q0, base, rows, tile):
    low_first = first_seen(meta, q0)
    low_last = first_seen(meta, q0 + BQ - 1)
    begin = jnp.maximum(low_first - base, 0) // BK
    end = jnp.minimum((WINDOW + q0 + BQ - 1 - base) // BK + 1, rows // BK)

    def step(t, carry):
        row = pl.multiple_of((end - 1 - t) * BK, BK)
        place = base + row
        plain = (place >= low_last) & (place + BK - 1 <= WINDOW + q0)

        @pl.when(plain)
        def _():
            tile(row, place, False)

        @pl.when(jnp.logical_not(plain))
        def _():
            tile(row, place, True)

        return carry

    lax.fori_loop(0, end - begin, step, 0)


def for_queries(tok, work):
    def step(t, carry):
        work(pl.multiple_of(t * BQ, BQ), pl.multiple_of(t * 2 * BQ, 2 * BQ))
        return carry

    lax.fori_loop(0, tok // BQ, step, 0)


def forward_tile(meta, q2, q0, k_ref, v_ref, m_ref, acc_ref, row, place, masked):
    k = k_ref[pl.ds(row, BK), :]
    v = v_ref[pl.ds(row, BK), :]
    s = lax.dot_general(k, q2, NT, preferred_element_type=F32)
    if masked:
        s = masked_tile(meta, s, q0, place)
    m_old = m_ref[0:1, :]
    m_new = jnp.maximum(m_old, jnp.max(s, axis=0, keepdims=True))
    p = jnp.exp2((s - m_new) * SCALE2)
    shrink = jnp.exp2((m_old - m_new) * SCALE2)
    v_ones = jnp.concatenate([v.T, jnp.ones((16, BK), BF16)], 0)
    acc_ref[...] = acc_ref[...] * shrink + lax.dot_general(
        v_ones, p.astype(BF16), NN, preferred_element_type=F32
    )
    m_ref[...] = jnp.broadcast_to(m_new, m_ref.shape)


def key_part(ref):
    return ref.at[:, 0:HEAD_DIM]


def value_part(ref):
    return ref.at[:, HEAD_DIM : 2 * HEAD_DIM]


def near_kernel(meta, q_ref, kv_ref, two_ref, odd_ref, m_out, acc_out, m_ref, acc_ref):
    tok = q_ref.shape[0]
    blocks = ((kv_ref, WINDOW), (two_ref, WINDOW - 2 * tok), (odd_ref, meta[8]))

    def work(q0, c0):
        q2 = heads_of(q_ref, q0)
        m_ref[...] = jnp.full(m_ref.shape, NEG, F32)
        acc_ref[...] = jnp.zeros(acc_ref.shape, F32)
        for ref, base in blocks:
            tile = functools.partial(
                forward_tile, meta, q2, q0, key_part(ref), value_part(ref), m_ref, acc_ref
            )
            for_tiles(meta, q0, base, tok, tile)
        m_out[:, pl.ds(c0, 2 * BQ)] = m_ref[...]
        acc_out[:, pl.ds(c0, 2 * BQ)] = acc_ref[...]

    for_queries(tok, work)


def far_kernel(meta, q_ref, four_ref, rest_ref, m_in, acc_in, o_ref, lse_ref, m_ref, acc_ref):
    tok = q_ref.shape[0]
    blocks = ((rest_ref, meta[9]), (four_ref, WINDOW - 4 * tok))

    def work(q0, c0):
        q2 = heads_of(q_ref, q0)
        m_ref[...] = m_in[:, pl.ds(c0, 2 * BQ)]
        acc_ref[...] = acc_in[:, pl.ds(c0, 2 * BQ)]
        for ref, base in blocks:
            tile = functools.partial(
                forward_tile, meta, q2, q0, key_part(ref), value_part(ref), m_ref, acc_ref
            )
            for_tiles(meta, q0, base, tok, tile)
        o = (acc_ref[0:HEAD_DIM, :] / acc_ref[HEAD_DIM : HEAD_DIM + 1, :]).T
        o_ref[pl.ds(q0, BQ), 0:HEAD_DIM] = o[:BQ].astype(BF16)
        o_ref[pl.ds(q0, BQ), HEAD_DIM : 2 * HEAD_DIM] = o[BQ:].astype(BF16)
        lse_ref[:, pl.ds(c0, 2 * BQ)] = m_ref[...] * SCALE2 + jnp.log2(
            acc_ref[HEAD_DIM : HEAD_DIM + 8, :]
        )

    for_queries(tok, work)


def call(kernel, name, n_vmem, out_shape, scratch, vmem_mb, cost=0):
    vmem = pl.BlockSpec(memory_space=pltpu.VMEM)
    return pl.pallas_call(
        kernel,
        out_shape=out_shape,
        in_specs=[pl.BlockSpec(memory_space=pltpu.SMEM)] + [vmem] * n_vmem,
        out_specs=jax.tree.map(lambda _: vmem, out_shape),
        scratch_shapes=scratch,
        compiler_params=pltpu.CompilerParams(vmem_limit_bytes=vmem_mb * 2**20),
        cost_estimate=pl.CostEstimate(flops=cost, bytes_accessed=0, transcendentals=0),
        name=name,
    )


def forward_scratch():
    return [pltpu.VMEM((8, 2 * BQ), F32), pltpu.VMEM((HEAD_DIM + 16, 2 * BQ), F32)]


def forward_near(meta, q, kv, two, odd):
    tok = q.shape[0]
    out = (
        jax.ShapeDtypeStruct((8, 2 * tok), F32),
        jax.ShapeDtypeStruct((HEAD_DIM + 16, 2 * tok), F32),
    )
    return call(near_kernel, "attn_near", 4, out, forward_scratch(), 24)(meta, q, kv, two, odd)


def forward_far(meta, q, four, rest, m, acc):
    tok = q.shape[0]
    out = (
        jax.ShapeDtypeStruct((tok, 2 * HEAD_DIM), BF16),
        jax.ShapeDtypeStruct((8, 2 * tok), F32),
    )
    return call(far_kernel, "attn_far", 5, out, forward_scratch(), 24)(meta, q, four, rest, m, acc)


def backward_kernel(bases, first, last, meta, q_ref, do_ref, o_ref, lse_ref, *refs):
    tok = q_ref.shape[0]
    n = len(bases)
    block_refs, refs = refs[:n], refs[n:]
    if not first:
        dqt_in, refs = refs[0], refs[1:]
    part_refs, dq_ref, (dqt, dk, dv) = refs[:n], refs[n], refs[n + 1 :]
    dk[...] = jnp.zeros(dk.shape, F32)
    dv[...] = jnp.zeros(dv.shape, F32)

    def work(q0, c0):
        cols = pl.ds(c0, 2 * BQ)
        q2 = heads_of(q_ref, q0)
        do2 = heads_of(do_ref, q0)
        o2 = heads_of(o_ref, q0)
        delta = jnp.sum((do2.astype(F32) * o2.astype(F32)).T, axis=0, keepdims=True)
        lse = lse_ref[0:1, cols]
        dqt[...] = jnp.zeros(dqt.shape, F32) if first else dqt_in[:, cols]

        def tile(index, row, place, masked):
            ref = block_refs[index]
            k = ref[pl.ds(row, BK), 0:HEAD_DIM]
            v = ref[pl.ds(row, BK), HEAD_DIM : 2 * HEAD_DIM]
            t = lax.dot_general(k, q2, NT, preferred_element_type=F32) * SCALE2 - lse
            if masked:
                t = masked_tile(meta, t, q0, place)
            p = jnp.exp2(t)
            dp = lax.dot_general(v, do2, NT, preferred_element_type=F32)
            ds = (p * (dp - delta)).astype(BF16)
            rows = pl.ds(row, BK)
            dv[index, rows, :] += lax.dot_general(
                p.astype(BF16), do2, NN, preferred_element_type=F32
            )
            dk[index, rows, :] += lax.dot_general(ds, q2, NN, preferred_element_type=F32)
            dqt[...] += lax.dot_general(k.T, ds, NN, preferred_element_type=F32)

        for index, base in enumerate(bases):
            base = base if base >= 0 else meta[-base]
            for_tiles(meta, q0, base, tok, functools.partial(tile, index))
        if last:
            dq = (dqt[...] * SCALE).T
            dq_ref[pl.ds(q0, BQ), 0:HEAD_DIM] = dq[:BQ].astype(BF16)
            dq_ref[pl.ds(q0, BQ), HEAD_DIM : 2 * HEAD_DIM] = dq[BQ:].astype(BF16)
        else:
            dq_ref[:, cols] = dqt[...]

    for_queries(tok, work)
    for index, ref in enumerate(part_refs):
        ref[:, 0:HEAD_DIM] = (dk[index] * SCALE).astype(ref.dtype)
        ref[:, HEAD_DIM : 2 * HEAD_DIM] = dv[index].astype(ref.dtype)


def backward(name, meta, common, blocks, bases, dqt=None, last=False):
    tok = common[0].shape[0]
    n = len(blocks)
    part = jax.ShapeDtypeStruct((tok, 2 * HEAD_DIM), F32 if last else BF16)
    dq = ((tok, 2 * HEAD_DIM), BF16) if last else ((HEAD_DIM, 2 * tok), F32)
    scratch = [
        pltpu.VMEM((HEAD_DIM, 2 * BQ), F32),
        pltpu.VMEM((n, tok, HEAD_DIM), F32),
        pltpu.VMEM((n, tok, HEAD_DIM), F32),
    ]
    args = list(common) + list(blocks) + ([] if dqt is None else [dqt])
    kernel = functools.partial(backward_kernel, bases, dqt is None, last)
    out = (part,) * n + (jax.ShapeDtypeStruct(*dq),)
    return call(kernel, name, len(args), out, scratch, 30)(meta, *args)


def projection_kernel(core, og_ref, wt_ref, attn_ref, d_attn_ref, mine_ref, other_ref, total, attn_t):
    step = pl.program_id(0)
    rows = mine_ref.shape[0] // 2

    @pl.when(step == 0)
    def _():
        total[...] = jnp.zeros(total.shape, F32)
        attn_t[...] = attn_ref[...].T

    og = og_ref[...]
    total[...] += lax.dot_general(og, wt_ref[...], NN, preferred_element_type=F32)
    dw = lax.dot_general(attn_t[...], og, NN, preferred_element_type=F32).T.astype(BF16)
    even = core[0] == 0
    for c in range(2):
        to = pl.ds(c * rows, rows)
        zero = dw[2 * c * rows : (2 * c + 1) * rows]
        one = dw[(2 * c + 1) * rows : (2 * c + 2) * rows]
        mine_ref[to, :] = jnp.where(even, zero, one)
        other_ref[to, :] = jnp.where(even, one, zero)

    @pl.when(step == pl.num_programs(0) - 1)
    def _():
        d_attn_ref[...] = total[...].astype(BF16)


def projection(core, out_grad, weight_t, attn, chunk):
    tok, width = out_grad.shape
    heads = attn.shape[1]
    whole = pl.BlockSpec((tok, heads), lambda i: (0, 0))
    half = pl.BlockSpec((chunk // 2, heads), lambda i: (i, 0))
    return pl.pallas_call(
        projection_kernel,
        grid=(width // chunk,),
        out_shape=(
            jax.ShapeDtypeStruct((tok, heads), BF16),
            jax.ShapeDtypeStruct((width // 2, heads), BF16),
            jax.ShapeDtypeStruct((width // 2, heads), BF16),
        ),
        in_specs=[
            pl.BlockSpec(memory_space=pltpu.SMEM),
            pl.BlockSpec((tok, chunk), lambda i: (0, i)),
            pl.BlockSpec((chunk, heads), lambda i: (i, 0)),
            whole,
        ],
        out_specs=(whole, half, half),
        scratch_shapes=[pltpu.VMEM((tok, heads), F32), pltpu.VMEM((heads, tok), BF16)],
        compiler_params=pltpu.CompilerParams(vmem_limit_bytes=24 * 2**20),
        cost_estimate=pl.CostEstimate(
            flops=1_000_000_000, bytes_accessed=1_000_000, transcendentals=0
        ),
        name="projection",
    )(core, out_grad, weight_t, attn)


def out_kernel(where, attn_ref, *refs):
    n = attn_ref.shape[0] // TOK
    weights, out_ref = refs[:n], refs[-1]
    cols = out_ref.shape[0]
    rows = pl.ds(pl.multiple_of(where[0] * cols, 16), cols)
    total = refs[n][...].astype(F32) if len(refs) == n + 2 else None
    for steps, w in enumerate(weights):
        origin = lax.rem(where[1] + n - steps, n)
        a = attn_ref[pl.ds(pl.multiple_of(origin * TOK, TOK), TOK), :]
        term = lax.dot_general(w[rows, :], a, NT, preferred_element_type=F32)
        total = term if total is None else total + term
    out_ref[...] = total.astype(BF16)


def out_part(name, where, attn_all, weights, extra=()):
    args = [attn_all] + list(weights) + list(extra)
    out = jax.ShapeDtypeStruct((weights[0].shape[0] // 2, TOK), BF16)
    return call(out_kernel, name, len(args), out, [], 24)(where, *args)


def ctx_shift(value, steps):
    count = lax.axis_size(CTX)
    leading, last = max(0, -steps), min(count, count - steps)
    return lax.ppermute(value, CTX, [(s, s + steps) for s in range(leading, last)])


def swap(value, axis):
    return lax.ppermute(value, axis, [(0, 1), (1, 0)])


def z_shift(value, steps):
    count = lax.axis_size("z")
    return lax.ppermute(value, "z", [(s, (s + steps) % count) for s in range(count)])


def body(query_rows, key_rows, value_rows, doc_ids, out_weight, out_grad):
    tok = query_rows.shape[0]
    core = lax.axis_index("core")
    even = core == 0
    z = lax.axis_index("z")
    xh = lax.axis_index("xh")
    n_z = lax.axis_size("z")

    weight_t = lax.all_gather(out_weight.T, CTX, axis=0, tiled=True)

    docs = lax.iota(jnp.int32, N_DOCS)
    count = jnp.sum((doc_ids[None, :] == docs[:, None]).astype(jnp.int32), axis=1)
    info = jnp.stack([count // 32, count % 32]).astype(BF16)
    info = jnp.pad(info, ((0, 14), (0, 2 * HEAD_DIM - N_DOCS)))
    kv = jnp.concatenate([jnp.concatenate([key_rows, value_rows], 1), info], 0)
    two = ctx_shift(kv, 2)
    four = ctx_shift(kv, 4)
    odd = swap(two, "core")

    def count_of(block):
        high, low = block[tok, :N_DOCS], block[tok + 1, :N_DOCS]
        return (high.astype(F32) * 32 + low.astype(F32)).astype(jnp.int32)

    local_start = jnp.cumsum(count) - count
    present = count > 0
    odd_base = jnp.where(even, WINDOW - tok, WINDOW - 3 * tok)
    rest_base = jnp.where(even, WINDOW - 3 * tok, WINDOW - tok)

    def meta_of(before):
        return jnp.concatenate(
            [
                jnp.where(present, local_start, FAR),
                jnp.where(present, WINDOW + local_start - before, 0),
                jnp.stack([odd_base, rest_base]).astype(jnp.int32),
            ]
        )

    between = jnp.where(even | (count_of(two) == 0), 0, tok)
    before_near = count_of(two) + count_of(odd)
    meta_near = meta_of(before_near + between)
    m, acc = forward_near(meta_near, query_rows, kv, two, odd)
    m, four, weight_t = lax.optimization_barrier((m, four, weight_t))
    rest = swap(jnp.where(even, kv, four), "core")
    meta = meta_of(before_near + count_of(four) + count_of(rest))
    attn, lse = forward_far(meta, query_rows, four, rest, m, acc)

    weight_z = weight_t.reshape(n_z, -1, weight_t.shape[1])

    def weight_for(steps):
        return lax.dynamic_index_in_dim(weight_z, (z + steps) % n_z, 0, keepdims=False)

    weights = [weight_for(0)] + [z_shift(weight_for(s), s) for s in range(1, n_z)]
    attn_all = lax.all_gather(attn, "z", axis=0, tiled=True)

    core_1 = core.reshape(1).astype(jnp.int32)
    d_attn, dw_mine, dw_other = projection(core_1, out_grad, weight_t, attn, weight_z.shape[1])
    dw_other = swap(dw_other, "core")
    dw = (dw_mine.astype(F32) + dw_other.astype(F32)).astype(BF16)
    dw = lax.psum_scatter(dw, ("xl", "y"), scatter_dimension=0, tiled=True)
    weight_grad = lax.optimization_barrier(dw.astype(F32)).T

    common = (query_rows, d_attn, attn, lse)
    rest_part, four_part, dqt = backward(
        "attn_back_far", meta, common, (rest, four), (-9, WINDOW - 4 * tok)
    )
    rest_part = swap(rest_part, "core").astype(F32)
    four_sum = (four_part.astype(F32) + jnp.where(even, 0.0, rest_part)).astype(BF16)
    out_other = out_part("out_other", jnp.stack([1 - xh, z]), attn_all, weights)
    dqt, four_sum, out_other = lax.optimization_barrier((dqt, four_sum, out_other))
    four_sum = ctx_shift(four_sum, -4)
    out_other = swap(out_other, "xh")

    odd_part, two_part, dqt = backward(
        "attn_back_mid", meta, common, (odd, two), (-8, WINDOW - 2 * tok), dqt
    )
    odd_part = swap(odd_part, "core").astype(F32)
    two_sum = (two_part.astype(F32) + odd_part).astype(BF16)
    dqt, two_sum = lax.optimization_barrier((dqt, two_sum))
    two_sum = ctx_shift(two_sum, -2)

    own, query_grad = backward("attn_back_own", meta, common, (kv,), (WINDOW,), dqt, last=True)
    layer_out = out_part("out_mine", jnp.stack([xh, z]), attn_all, weights, (out_other,)).T

    own = own + jnp.where(even, rest_part, 0.0)
    own = (own + four_sum.astype(F32) + two_sum.astype(F32)).astype(BF16)
    return layer_out, query_grad, own[:, :HEAD_DIM], own[:, HEAD_DIM:], weight_grad


def solution(mesh):
    fine = Mesh(mesh.devices.reshape(2, 4, 2, 4, 2), CTX + FSDP)
    in_specs = (
        P(CTX, FSDP),
        P(CTX, FSDP),
        P(CTX, FSDP),
        P(CTX),
        P(FSDP, CTX),
        P(CTX, None),
    )
    out_specs = (
        P(CTX, FSDP),
        P(CTX, FSDP),
        P(CTX, FSDP),
        P(CTX, FSDP),
        P(FSDP, CTX),
    )
    return jax.shard_map(body, mesh=fine, in_specs=in_specs, out_specs=out_specs, check_vma=False)
```

time: 216 us -> 228 us (1.056)
  the two profiles are of different devices: /device:TPU:52 before, /device:TPU:25 now
where the time goes in v1:
time: 228 us; the launch traced here: 224 us
  waiting for transfers between devices  95.6 us (42%)
  Pallas kernels  47.2 us (21%)
  starting transfers between devices  39.3 us (17%)
  local copies, waits for them, and re-layouts  17.2 us (8%)
  between operations  14.3 us (6%)
  other arithmetic  10.6 us (5%)
    ppermute x4, waiting for transfers between devices, ctx_shift(): lax.ppermute(value, CTX, [(s, s + steps) for s in range(leading, last)])  56.9 us
    ppermute x3, waiting for transfers between devices, z_shift(): lax.ppermute(value, 'z', [(s, (s + steps) % count) for s in range(count)])  29.2 us
    ppermute x4, starting transfers between devices, ctx_shift(): lax.ppermute(value, CTX, [(s, s + steps) for s in range(leading, last)])  23.4 us
    pallas_call x3, Pallas kernels, backward(): return call(kernel, name, len(args), out, scratch, 30)(meta, *args)  19.6 us
    unnamed x60, local copies, waits for them, and re-layouts  15 us
    ppermute x6, starting transfers between devices, swap(): return lax.ppermute(value, axis, [(0, 1), (1, 0)])  10.1 us
    pallas_call x1, Pallas kernels, projection(): pl.pallas_call(projection_kernel, grid=(width // chunk,), out_shape=(jax....  8.35 us
    pallas_call x1, Pallas kernels, forward_near(): call(near_kernel, 'attn_near', 4, out, forward_scratch(), 24)  7.84 us
  transfers between devices with their start and end apart: 16, of which 9 were waited for; matrix products, arithmetic and copies ran while one was open for 6% of the time, Pallas kernels for 17%

profile of v1, /device:TPU:25, one launch (start us, length us, event | category | flops | bytes accessed | tf_op | source)
XLA Modules:
  0.0 224.2 jit_solution(15987436151448285509)
XLA Ops:
  8.0 0.8 convert_reduce_fusion
  8.8 1.1 pad_maximum_fusion.kv_ref.refs_0_
  9.9 2.9 %collective-permute-start = (bf16[1040,256]{1,0:T(8,128)(2,1)S(1)}, bf16[1040,256]{1,0:T(8,128)(2,1)S(1)}, u32[]{:S(2)}, u32[]{:S(2)}) collective-permute-start(bf16[1040,256]{1,0:T(8,128)(2,1)S(1)} %pad_maximum_fusion.kv_ref.refs_0_), channel_id=1, source_target_pairs={{0,16},{8,24},{16,32},{24,40},{32,48},{40,56},{48,64},{56,72},{64,... | collective-permute-start | bytes 1597448 | tf_op jit(solution)/shard_map/ppermute | solution.py:334
  12.8 14.3 %collective-permute-done.two_ref.refs_1_ = bf16[1040,256]{1,0:T(8,128)(2,1)S(1)} collective-permute-done((bf16[1040,256]{1,0:T(8,128)(2,1)S(1)}, bf16[1040,256]{1,0:T(8,128)(2,1)S(1)}, u32[]{:S(2)}, u32[]{:S(2)}) %collective-permute-start) | collective-permute-done | bytes 532512 | tf_op jit(solution)/shard_map/ppermute | solution.py:334
  27.1 2.9 %collective-permute-start.1 = (bf16[1040,256]{1,0:T(8,128)(2,1)S(1)}, bf16[1040,256]{1,0:T(8,128)(2,1)S(1)}, u32[]{:S(2)}, u32[]{:S(2)}) collective-permute-start(bf16[1040,256]{1,0:T(8,128)(2,1)S(1)} %collective-permute-done.two_ref.refs_1_), channel_id=1, source_target_pairs={{0,8},{8,0},{1,9},{9,1},{2,10},{10,2},{3,11},{11,3},{4,12},{12,4},... | collective-permute-start | bytes 1597448 | tf_op jit(solution)/shard_map/ppermute | solution.py:338
  30.0 4.2 %collective-permute-start.2 = (bf16[1040,256]{1,0:T(8,128)(2,1)S(1)}, bf16[1040,256]{1,0:T(8,128)(2,1)S(1)}, u32[]{:S(2)}, u32[]{:S(2)}) collective-permute-start(bf16[1040,256]{1,0:T(8,128)(2,1)S(1)} %pad_maximum_fusion.kv_ref.refs_0_), channel_id=1, source_target_pairs={{0,32},{8,40},{16,48},{24,56},{32,64},{40,72},{48,80},{56,88},{64,... | collective-permute-start | bytes 1597448 | tf_op jit(solution)/shard_map/ppermute | solution.py:334
  34.5 7.8 %attn_near.1 = (f32[8,2048]{1,0:T(8,128)S(1)}, f32[144,2048]{1,0:T(8,128)S(1)}) custom-call(s32[10]{0:T(128)S(1)} %add_add_fusion.meta, bf16[1024,256]{1,0:T(8,128)(2,1)S(1)} %copy-done, bf16[1040,256]{1,0:T(8,128)(2,1)S(1)} %pad_maximum_fusion.kv_ref.refs_0_, bf16[1040,256]{1,0:T(8,128)(2,1)S(1)} %collective-permute-done.two_ref.refs_1_, ...), custom_call_target="tpu_custom_call" | custom-call | tf_op jit(solution)/shard_map/attn_near/pallas_call | solution.py:177
  42.4 1.0 copy-done.19
  43.4 8.1 %collective-permute-done.2.four_ref.refs_1_ = bf16[1040,256]{1,0:T(8,128)(2,1)S(1)} collective-permute-done((bf16[1040,256]{1,0:T(8,128)(2,1)S(1)}, bf16[1040,256]{1,0:T(8,128)(2,1)S(1)}, u32[]{:S(2)}, u32[]{:S(2)}) %collective-permute-start.2) | collective-permute-done | bytes 532512 | tf_op jit(solution)/shard_map/ppermute | solution.py:334
  51.5 4.1 %all-gather.3.cloned.1.call-done.wt_ref = bf16[4608,256]{1,0:T(8,128)(2,1)} async-done(((bf16[288,256]{1,0:T(8,128)(2,1)}), bf16[4608,256]{1,0:T(8,128)(2,1)}) %all-gather.3.cloned.1.call-update) | async-done | bytes 2359312 | tf_op jit(solution)/shard_map/all_gather | solution.py:354
  55.8 0.9 collective-permute-start.3
  56.7 1.7 collective-permute-done.3.rest_ref.refs_0_
  58.5 0.9 copy-done.27
  59.4 4.6 %attn_far.1 = (bf16[1024,256]{1,0:T(8,128)(2,1)}, f32[8,2048]{1,0:T(8,128)S(1)}) custom-call(s32[10]{0:T(128)S(1)} %add_add_fusion.1.meta, bf16[1024,256]{1,0:T(8,128)(2,1)S(1)} %copy-done, bf16[1040,256]{1,0:T(8,128)(2,1)S(1)} %collective-permute-done.2.four_ref.refs_1_, bf16[1040,256]{1,0:T(8,128)(2,1)S(1)} %collective-permute-done.3.rest_ref.refs_0_, ...), custom_call_target="tpu_custom_call" | custom-call | tf_op jit(solution)/shard_map/attn_far/pallas_call | solution.py:186
  64.1 3.7 %copy-done.1 = bf16[1024,4608]{1,0:T(8,128)(2,1)S(1)} copy-done((bf16[1024,4608]{1,0:T(8,128)(2,1)S(1)}, bf16[1024,4608]{1,0:T(8,128)(2,1)}, u32[]{:S(2)}) %copy-start.1) | copy-done | bytes 9437208
  67.8 8.3 %projection.1 = (bf16[1024,256]{1,0:T(8,128)(2,1)S(1)}, bf16[2304,256]{1,0:T(8,128)(2,1)S(1)}, bf16[2304,256]{1,0:T(8,128)(2,1)S(1)}) custom-call(s32[1]{0:T(128)} %bitcast.15.core, bf16[1024,4608]{1,0:T(8,128)(2,1)S(1)} %copy-done.1, bf16[4608,256]{1,0:T(8,128)(2,1)S(1)} %copy-done.2, bf16[1024,256]{1,0:T(8,128)(2,1)} %get-tuple-element.32.attn_ref.o_ref), custom_call_target="tpu_custom_call" | custom-call | flops 1000000000 | bytes 1000000 | tf_op jit(solution)/shard_map/projection/pallas_call | solution.py:287
  76.1 0.8 copy-done.7
  77.1 2.8 %collective-permute-done.12 = bf16[2304,256]{1,0:T(8,128)(2,1)S(1)} collective-permute-done((bf16[2304,256]{1,0:T(8,128)(2,1)S(1)}, bf16[2304,256]{1,0:T(8,128)(2,1)S(1)}, u32[]{:S(2)}, u32[]{:S(2)}) %collective-permute-start.12) | collective-permute-done | bytes 1179680 | tf_op jit(solution)/shard_map/ppermute | solution.py:338
  79.9 1.4 add_convert_fusion
  81.4 1.1 copy-done.8
  82.5 1.1 copy-done.18
  83.6 6.2 %attn_back_far.1 = (bf16[1024,256]{1,0:T(8,128)(2,1)}, bf16[1024,256]{1,0:T(8,128)(2,1)S(1)}, f32[128,2048]{1,0:T(8,128)S(1)}) custom-call(s32[10]{0:T(128)S(1)} %add_add_fusion.1.meta, bf16[1024,256]{1,0:T(8,128)(2,1)S(1)} %copy-done, bf16[1024,256]{1,0:T(8,128)(2,1)S(1)} %copy-done.8, bf16[1024,256]{1,0:T(8,128)(2,1)} %get-tuple-element.32.attn_ref.o_ref, ...), custom_call_target="tpu_custom_call" | custom-call | tf_op jit(solution)/shard_map/attn_back_far/pallas_call | solution.py:254
  89.8 1.4 dynamic-slice_bitcast_fusion
  91.4 1.5 collective-permute-start.4
  92.9 3.2 %collective-permute-start.5 = (bf16[1152,256]{1,0:T(8,128)(2,1)}, bf16[1152,256]{1,0:T(8,128)(2,1)S(1)}, u32[]{:S(2)}, u32[]{:S(2)}) collective-permute-start(bf16[1152,256]{1,0:T(8,128)(2,1)} %get-tuple-element.52), channel_id=1, source_target_pairs={{0,4},{2,6},{4,0},{6,2},{1,5},{3,7},{5,1},{7,3},{8,12},{10,14},{12... | collective-permute-start | bytes 1769480 | tf_op jit(solution)/shard_map/ppermute | solution.py:343
  96.1 1.0 collective-permute-start.6
  97.2 2.2 fusion.1
  99.4 16.5 %collective-permute-done.4.refs_1_ = bf16[1152,256]{1,0:T(8,128)(2,1)S(1)} collective-permute-done((bf16[1152,256]{1,0:T(8,128)(2,1)}, bf16[1152,256]{1,0:T(8,128)(2,1)S(1)}, u32[]{:S(2)}, u32[]{:S(2)}) %collective-permute-start.4) | collective-permute-done | bytes 589856 | tf_op jit(solution)/shard_map/ppermute | solution.py:343
  115.9 12.7 %collective-permute-done.5.refs_2_ = bf16[1152,256]{1,0:T(8,128)(2,1)S(1)} collective-permute-done((bf16[1152,256]{1,0:T(8,128)(2,1)}, bf16[1152,256]{1,0:T(8,128)(2,1)S(1)}, u32[]{:S(2)}, u32[]{:S(2)}) %collective-permute-start.5) | collective-permute-done | bytes 589856 | tf_op jit(solution)/shard_map/ppermute | solution.py:343
  128.6 0.8 copy-done.10
  129.5 1.6 copy-done.3
  131.1 1.1 copy-done.11
  132.1 3.0 %out_other.1 = bf16[576,1024]{1,0:T(8,128)(2,1)} custom-call(s32[2]{0:T(128)S(1)} %pad_add_fusion.1.where, bf16[4096,256]{1,0:T(8,128)(2,1)S(1)} %copy-done.3, bf16[1152,256]{1,0:T(8,128)(2,1)S(1)} %get-tuple-element.54.refs_0_, bf16[1152,256]{1,0:T(8,128)(2,1)S(1)} %collective-permute-done.4.refs_1_, bf16[1152,256]{1,0:T(8,128)(2,1)S(1)} %collective-permute-done.5.refs_2_, ...), custom_call_target="tpu_custom_call" | custom-call | tf_op jit(solution)/shard_map/out_other/pallas_call | solution.py:328
  135.1 5.5 %attn_back_mid.1 = (bf16[1024,256]{1,0:T(8,128)(2,1)S(1)}, bf16[1024,256]{1,0:T(8,128)(2,1)S(1)}, f32[128,2048]{1,0:T(8,128)S(1)}) custom-call(s32[10]{0:T(128)S(1)} %add_add_fusion.1.meta, bf16[1024,256]{1,0:T(8,128)(2,1)S(1)} %copy-done, bf16[1024,256]{1,0:T(8,128)(2,1)S(1)} %copy-done.9, bf16[1024,256]{1,0:T(8,128)(2,1)} %get-tuple-element.32.attn_ref.o_ref, ...), custom_call_target="tpu_custom_call" | custom-call | tf_op jit(solution)/shard_map/attn_back_mid/pallas_call | solution.py:254
  140.7 1.0 copy-done.21
  141.7 3.5 %collective-permute-start.9 = (bf16[1024,256]{1,0:T(8,128)(2,1)S(1)}, bf16[1024,256]{1,0:T(8,128)(2,1)S(1)}, u32[]{:S(2)}, u32[]{:S(2)}) collective-permute-start(bf16[1024,256]{1,0:T(8,128)(2,1)S(1)} %get-tuple-element.43), channel_id=1, source_target_pairs={{0,8},{8,0},{1,9},{9,1},{2,10},{10,2},{3,11},{11,3},{4,12},{12,4},... | collective-permute-start | bytes 1572872 | tf_op jit(solution)/shard_map/ppermute | solution.py:338
  145.1 2.7 %collective-permute-start.8 = (bf16[576,1024]{1,0:T(8,128)(2,1)}, bf16[576,1024]{1,0:T(8,128)(2,1)}, u32[]{:S(2)}, u32[]{:S(2)}) collective-permute-start(bf16[576,1024]{1,0:T(8,128)(2,1)} %out_other.1), channel_id=1, source_target_pairs={{0,1},{1,0},{2,3},{3,2},{4,5},{5,4},{6,7},{7,6},{8,9},{9,8},{10,11... | collective-permute-start | bytes 3538952 | tf_op jit(solution)/shard_map/ppermute | solution.py:338
  147.8 8.1 %collective-permute-start.10 = (bf16[1024,256]{1,0:T(8,128)(2,1)}, bf16[1024,256]{1,0:T(8,128)(2,1)}, u32[]{:S(2)}, u32[]{:S(2)}) collective-permute-start(bf16[1024,256]{1,0:T(8,128)(2,1)} %fusion.1), channel_id=1, source_target_pairs={{32,0},{40,8},{48,16},{56,24},{64,32},{72,40},{80,48},{88,56},{96,... | collective-permute-start | bytes 1572872 | tf_op jit(solution)/shard_map/ppermute | solution.py:334
  156.0 1.0 add_convert_fusion.1
  157.0 8.2 %collective-permute-start.11 = (bf16[1024,256]{1,0:T(8,128)(2,1)}, bf16[1024,256]{1,0:T(8,128)(2,1)}, u32[]{:S(2)}, u32[]{:S(2)}) collective-permute-start(bf16[1024,256]{1,0:T(8,128)(2,1)} %add_convert_fusion.1), channel_id=1, source_target_pairs={{16,0},{24,8},{32,16},{40,24},{48,32},{56,40},{64,48},{72,56},{80,... | collective-permute-start | bytes 1572872 | tf_op jit(solution)/shard_map/ppermute | solution.py:334
  165.2 1.6 convert_element_type.133
  166.9 1.2 copy-done.22
  168.1 7.9 %attn_back_own.1 = (f32[1024,256]{1,0:T(8,128)S(1)}, bf16[1024,256]{1,0:T(8,128)(2,1)}) custom-call(s32[10]{0:T(128)S(1)} %add_add_fusion.1.meta, bf16[1024,256]{1,0:T(8,128)(2,1)S(1)} %copy-done, bf16[1024,256]{1,0:T(8,128)(2,1)S(1)} %copy-done.9, bf16[1024,256]{1,0:T(8,128)(2,1)} %get-tuple-element.32.attn_ref.o_ref, ...), custom_call_target="tpu_custom_call" | custom-call | tf_op jit(solution)/shard_map/attn_back_own/pallas_call | solution.py:254
  176.0 30.5 %collective-permute-done.10 = bf16[1024,256]{1,0:T(8,128)(2,1)} collective-permute-done((bf16[1024,256]{1,0:T(8,128)(2,1)}, bf16[1024,256]{1,0:T(8,128)(2,1)}, u32[]{:S(2)}, u32[]{:S(2)}) %collective-permute-start.10) | collective-permute-done | bytes 524320 | tf_op jit(solution)/shard_map/ppermute | solution.py:334
  206.5 4.1 %collective-permute-done.11 = bf16[1024,256]{1,0:T(8,128)(2,1)} collective-permute-done((bf16[1024,256]{1,0:T(8,128)(2,1)}, bf16[1024,256]{1,0:T(8,128)(2,1)}, u32[]{:S(2)}, u32[]{:S(2)}) %collective-permute-start.11) | collective-permute-done | bytes 524320 | tf_op jit(solution)/shard_map/ppermute | solution.py:334
  210.5 1.8 fusion.5
  212.3 0.8 fusion.28
  213.7 3.7 %out_mine.1 = bf16[576,1024]{1,0:T(8,128)(2,1)} custom-call(s32[2]{0:T(128)S(1)} %pad_add_fusion.where, bf16[4096,256]{1,0:T(8,128)(2,1)S(1)} %copy-done.4, bf16[1152,256]{1,0:T(8,128)(2,1)S(1)} %get-tuple-element.54.refs_0_, bf16[1152,256]{1,0:T(8,128)(2,1)S(1)} %collective-permute-done.4.refs_1_, bf16[1152,256]{1,0:T(8,128)(2,1)S(1)} %collective-permute-done.5.refs_2_, ...), custom_call_target="tpu_custom_call" | custom-call | tf_op jit(solution)/shard_map/out_mine/pallas_call | solution.py:328
  (74 shorter events, 2.5 us)
Async XLA Ops:
  7.2 27.3 %copy-start = (bf16[1024,256]{1,0:T(8,128)(2,1)S(1)}, bf16[1024,256]{1,0:T(8,128)(2,1)}, u32[]{:S(2)}) copy-start(bf16[1024,256]{1,0:T(8,128)(2,1)} %q_ref.9) | copy-start | bytes 1572868
  7.2 48.4 %all-gather.3.cloned.1.call-start = ((), (), s32[]{:S(2)}) async-start(), calls=%async_computation.1 | async-start | bytes 2506752 | tf_op jit(solution)/shard_map/all_gather | solution.py:354
  7.9 121.6 %all-gather.5.cloned.1.call-start = ((), (), s32[]{:S(2)}) async-start(), calls=%async_computation.2 | async-start | bytes 2621440 | tf_op jit(solution)/shard_map/all_gather | solution.py:398
  9.9 45.9 %copy-start.5 = (bf16[1040,256]{1,0:T(8,128)(2,1)}, bf16[1040,256]{1,0:T(8,128)(2,1)S(1)}, u32[]{:S(2)}) copy-start(bf16[1040,256]{1,0:T(8,128)(2,1)S(1)} %pad_maximum_fusion.kv_ref.refs_0_) | copy-start | bytes 1597444
  9.9 45.7 %copy-start.28 = (bf16[1024,128]{1,0:T(8,128)(2,1)S(1)}, bf16[1024,128]{1,0:T(8,128)(2,1)}, u32[]{:S(2)}) copy-start(bf16[1024,128]{1,0:T(8,128)(2,1)} %param.8) | copy-start | bytes 786436
  9.9 45.7 %copy-start.29 = (bf16[1024,128]{1,0:T(8,128)(2,1)S(1)}, bf16[1024,128]{1,0:T(8,128)(2,1)}, u32[]{:S(2)}) copy-start(bf16[1024,128]{1,0:T(8,128)(2,1)} %param.7) | copy-start | bytes 786436
  9.9 17.2 %collective-permute-start = (bf16[1040,256]{1,0:T(8,128)(2,1)S(1)}, bf16[1040,256]{1,0:T(8,128)(2,1)S(1)}, u32[]{:S(2)}, u32[]{:S(2)}) collective-permute-start(bf16[1040,256]{1,0:T(8,128)(2,1)S(1)} %pad_maximum_fusion.kv_ref.refs_0_), channel_id=1, source_target_pairs={{0,16},{8,24},{16,32},{24,40},{32,48},{40,56},{48,64},{56,72},{64,... | collective-permute-start | bytes 1597448 | tf_op jit(solution)/shard_map/ppermute | solution.py:334
  27.1 31.2 %copy-start.13 = (bf16[1040,256]{1,0:T(8,128)(2,1)}, bf16[1040,256]{1,0:T(8,128)(2,1)S(1)}, u32[]{:S(2)}) copy-start(bf16[1040,256]{1,0:T(8,128)(2,1)S(1)} %collective-permute-done.two_ref.refs_1_) | copy-start | bytes 1597444
  27.1 7.3 %collective-permute-start.1 = (bf16[1040,256]{1,0:T(8,128)(2,1)S(1)}, bf16[1040,256]{1,0:T(8,128)(2,1)S(1)}, u32[]{:S(2)}, u32[]{:S(2)}) collective-permute-start(bf16[1040,256]{1,0:T(8,128)(2,1)S(1)} %collective-permute-done.two_ref.refs_1_), channel_id=1, source_target_pairs={{0,8},{8,0},{1,9},{9,1},{2,10},{10,2},{3,11},{11,3},{4,12},{12,4},... | collective-permute-start | bytes 1597448 | tf_op jit(solution)/shard_map/ppermute | solution.py:338
  30.0 21.5 %collective-permute-start.2 = (bf16[1040,256]{1,0:T(8,128)(2,1)S(1)}, bf16[1040,256]{1,0:T(8,128)(2,1)S(1)}, u32[]{:S(2)}, u32[]{:S(2)}) collective-permute-start(bf16[1040,256]{1,0:T(8,128)(2,1)S(1)} %pad_maximum_fusion.kv_ref.refs_0_), channel_id=1, source_target_pairs={{0,32},{8,40},{16,48},{24,56},{32,64},{40,72},{48,80},{56,88},{64,... | collective-permute-start | bytes 1597448 | tf_op jit(solution)/shard_map/ppermute | solution.py:334
  34.4 23.9 %copy-start.15 = (bf16[1040,256]{1,0:T(8,128)(2,1)}, bf16[1040,256]{1,0:T(8,128)(2,1)S(1)}, u32[]{:S(2)}) copy-start(bf16[1040,256]{1,0:T(8,128)(2,1)S(1)} %collective-permute-done.1.odd_ref.refs_0_) | copy-start | bytes 1597444
  42.4 1.0 copy-start.19
  43.4 15.1 %copy-start.26 = (f32[8,2048]{1,0:T(8,128)}, f32[8,2048]{1,0:T(8,128)S(1)}, u32[]{:S(2)}) copy-start(f32[8,2048]{1,0:T(8,128)S(1)} %get-tuple-element.30.m_in) | copy-start | bytes 196612
  55.6 2.8 %copy-start.20 = (f32[144,2048]{1,0:T(8,128)S(1)}, f32[144,2048]{1,0:T(8,128)}, u32[]{:S(2)}) copy-start(f32[144,2048]{1,0:T(8,128)} %copy-done.19) | copy-start | bytes 3538948
  55.8 2.5 %collective-permute-start.3 = (bf16[1040,256]{1,0:T(8,128)(2,1)S(1)}, bf16[1040,256]{1,0:T(8,128)(2,1)S(1)}, u32[]{:S(2)}, u32[]{:S(2)}) collective-permute-start(bf16[1040,256]{1,0:T(8,128)(2,1)S(1)} %broadcast_select_fusion), channel_id=1, source_target_pairs={{0,8},{8,0},{1,9},{9,1},{2,10},{10,2},{3,11},{11,3},{4,12},{12,4},... | collective-permute-start | bytes 1597448 | tf_op jit(solution)/shard_map/ppermute | solution.py:338
  58.3 5.7 %copy-start.17 = (bf16[1040,256]{1,0:T(8,128)(2,1)}, bf16[1040,256]{1,0:T(8,128)(2,1)S(1)}, u32[]{:S(2)}) copy-start(bf16[1040,256]{1,0:T(8,128)(2,1)S(1)} %collective-permute-done.3.rest_ref.refs_0_) | copy-start | bytes 1597444
  58.5 0.9 copy-start.27
  59.4 4.7 %copy-start.2 = (bf16[4608,256]{1,0:T(8,128)(2,1)S(1)}, bf16[4608,256]{1,0:T(8,128)(2,1)}, u32[]{:S(2)}) copy-start(bf16[4608,256]{1,0:T(8,128)(2,1)} %all-gather.3.cloned.1.call-done.wt_ref) | copy-start | bytes 7077892
  64.0 101.2 %reduce-scatter.2.cloned.1.call-start = ((), (), s32[]{:S(2)}) async-start(), calls=%async_computation.3 | async-start | bytes 1327104 | tf_op jit(solution)/shard_map/reduce_scatter | solution.py:404
  64.1 3.7 %copy-start.1 = (bf16[1024,4608]{1,0:T(8,128)(2,1)S(1)}, bf16[1024,4608]{1,0:T(8,128)(2,1)}, u32[]{:S(2)}) copy-start(bf16[1024,4608]{1,0:T(8,128)(2,1)} %og_ref.1) | copy-start | bytes 28311556
  76.1 0.8 copy-start.7
  76.9 3.0 %collective-permute-start.12 = (bf16[2304,256]{1,0:T(8,128)(2,1)S(1)}, bf16[2304,256]{1,0:T(8,128)(2,1)S(1)}, u32[]{:S(2)}, u32[]{:S(2)}) collective-permute-start(bf16[2304,256]{1,0:T(8,128)(2,1)S(1)} %get-tuple-element.50), channel_id=1, source_target_pairs={{0,8},{8,0},{1,9},{9,1},{2,10},{10,2},{3,11},{11,3},{4,12},{12,4},... | collective-permute-start | bytes 3538952 | tf_op jit(solution)/shard_map/ppermute | solution.py:338
  81.4 1.1 copy-start.8
  82.5 1.1 copy-start.18
  89.8 1.6 copy-start.23
  89.8 6.3 %copy-start.25 = (bf16[1024,256]{1,0:T(8,128)(2,1)}, bf16[1024,256]{1,0:T(8,128)(2,1)S(1)}, u32[]{:S(2)}) copy-start(bf16[1024,256]{1,0:T(8,128)(2,1)S(1)} %get-tuple-element.37) | copy-start | bytes 1572868
  89.8 7.4 %collective-permute-start.7 = (bf16[1024,256]{1,0:T(8,128)(2,1)}, bf16[1024,256]{1,0:T(8,128)(2,1)}, u32[]{:S(2)}, u32[]{:S(2)}) collective-permute-start(bf16[1024,256]{1,0:T(8,128)(2,1)} %get-tuple-element.38), channel_id=1, source_target_pairs={{0,8},{8,0},{1,9},{9,1},{2,10},{10,2},{3,11},{11,3},{4,12},{12,4},... | collective-permute-start | bytes 1572872 | tf_op jit(solution)/shard_map/ppermute | solution.py:338
  91.4 24.5 %collective-permute-start.4 = (bf16[1152,256]{1,0:T(8,128)(2,1)}, bf16[1152,256]{1,0:T(8,128)(2,1)S(1)}, u32[]{:S(2)}, u32[]{:S(2)}) collective-permute-start(bf16[1152,256]{1,0:T(8,128)(2,1)} %get-tuple-element.53), channel_id=1, source_target_pairs={{0,2},{2,4},{4,6},{6,0},{1,3},{3,5},{5,7},{7,1},{8,10},{10,12},{12... | collective-permute-start | bytes 1769480 | tf_op jit(solution)/shard_map/ppermute | solution.py:343
  92.9 35.7 %collective-permute-start.5 = (bf16[1152,256]{1,0:T(8,128)(2,1)}, bf16[1152,256]{1,0:T(8,128)(2,1)S(1)}, u32[]{:S(2)}, u32[]{:S(2)}) collective-permute-start(bf16[1152,256]{1,0:T(8,128)(2,1)} %get-tuple-element.52), channel_id=1, source_target_pairs={{0,4},{2,6},{4,0},{6,2},{1,5},{3,7},{5,1},{7,3},{8,12},{10,14},{12... | collective-permute-start | bytes 1769480 | tf_op jit(solution)/shard_map/ppermute | solution.py:343
  96.1 32.5 %collective-permute-start.6 = (bf16[1152,256]{1,0:T(8,128)(2,1)}, bf16[1152,256]{1,0:T(8,128)(2,1)S(1)}, u32[]{:S(2)}, u32[]{:S(2)}) collective-permute-start(bf16[1152,256]{1,0:T(8,128)(2,1)} %get-tuple-element.51), channel_id=1, source_target_pairs={{0,6},{2,0},{4,2},{6,4},{1,7},{3,1},{5,3},{7,5},{8,14},{10,8},{12,... | collective-permute-start | bytes 1769480 | tf_op jit(solution)/shard_map/ppermute | solution.py:343
  128.6 0.8 copy-start.10
  129.5 1.6 copy-start.3
  131.1 1.1 copy-start.11
  132.1 3.0 %copy-start.9 = (bf16[1024,256]{1,0:T(8,128)(2,1)S(1)}, bf16[1024,256]{1,0:T(8,128)(2,1)}, u32[]{:S(2)}) copy-start(bf16[1024,256]{1,0:T(8,128)(2,1)} %copy-done.7) | copy-start | bytes 1572868
  132.1 3.0 %copy-start.14 = (bf16[1040,256]{1,0:T(8,128)(2,1)S(1)}, bf16[1040,256]{1,0:T(8,128)(2,1)}, u32[]{:S(2)}) copy-start(bf16[1040,256]{1,0:T(8,128)(2,1)} %copy-done.13) | copy-start | bytes 1597444
  132.1 3.0 %copy-start.16 = (bf16[1040,256]{1,0:T(8,128)(2,1)S(1)}, bf16[1040,256]{1,0:T(8,128)(2,1)}, u32[]{:S(2)}) copy-start(bf16[1040,256]{1,0:T(8,128)(2,1)} %copy-done.15) | copy-start | bytes 1597444
  132.1 3.0 %copy-start.24 = (f32[128,2048]{1,0:T(8,128)S(1)}, f32[128,2048]{1,0:T(8,128)}, u32[]{:S(2)}) copy-start(f32[128,2048]{1,0:T(8,128)} %copy-done.23) | copy-start | bytes 3145732
  140.7 1.0 copy-start.21
  141.7 25.2 %copy-start.6 = (bf16[1040,256]{1,0:T(8,128)(2,1)S(1)}, bf16[1040,256]{1,0:T(8,128)(2,1)}, u32[]{:S(2)}) copy-start(bf16[1040,256]{1,0:T(8,128)(2,1)} %copy-done.5) | copy-start | bytes 1597444
  141.7 14.3 %collective-permute-start.9 = (bf16[1024,256]{1,0:T(8,128)(2,1)S(1)}, bf16[1024,256]{1,0:T(8,128)(2,1)S(1)}, u32[]{:S(2)}, u32[]{:S(2)}) collective-permute-start(bf16[1024,256]{1,0:T(8,128)(2,1)S(1)} %get-tuple-element.43), channel_id=1, source_target_pairs={{0,8},{8,0},{1,9},{9,1},{2,10},{10,2},{3,11},{11,3},{4,12},{12,4},... | collective-permute-start | bytes 1572872 | tf_op jit(solution)/shard_map/ppermute | solution.py:338
  145.1 68.0 %collective-permute-start.8 = (bf16[576,1024]{1,0:T(8,128)(2,1)}, bf16[576,1024]{1,0:T(8,128)(2,1)}, u32[]{:S(2)}, u32[]{:S(2)}) collective-permute-start(bf16[576,1024]{1,0:T(8,128)(2,1)} %out_other.1), channel_id=1, source_target_pairs={{0,1},{1,0},{2,3},{3,2},{4,5},{5,4},{6,7},{7,6},{8,9},{9,8},{10,11... | collective-permute-start | bytes 3538952 | tf_op jit(solution)/shard_map/ppermute | solution.py:338
  147.8 58.6 %collective-permute-start.10 = (bf16[1024,256]{1,0:T(8,128)(2,1)}, bf16[1024,256]{1,0:T(8,128)(2,1)}, u32[]{:S(2)}, u32[]{:S(2)}) collective-permute-start(bf16[1024,256]{1,0:T(8,128)(2,1)} %fusion.1), channel_id=1, source_target_pairs={{32,0},{40,8},{48,16},{56,24},{64,32},{72,40},{80,48},{88,56},{96,... | collective-permute-start | bytes 1572872 | tf_op jit(solution)/shard_map/ppermute | solution.py:334
  157.0 53.6 %collective-permute-start.11 = (bf16[1024,256]{1,0:T(8,128)(2,1)}, bf16[1024,256]{1,0:T(8,128)(2,1)}, u32[]{:S(2)}, u32[]{:S(2)}) collective-permute-start(bf16[1024,256]{1,0:T(8,128)(2,1)} %add_convert_fusion.1), channel_id=1, source_target_pairs={{16,0},{24,8},{32,16},{40,24},{48,32},{56,40},{64,48},{72,56},{80,... | collective-permute-start | bytes 1572872 | tf_op jit(solution)/shard_map/ppermute | solution.py:334
  166.9 1.2 copy-start.22
  210.5 2.6 %copy-start.4 = (bf16[4096,256]{1,0:T(8,128)(2,1)S(1)}, bf16[4096,256]{1,0:T(8,128)(2,1)}, u32[]{:S(2)}) copy-start(bf16[4096,256]{1,0:T(8,128)(2,1)} %all-gather.5.cloned.1.call-done.attn_ref) | copy-start | bytes 6291460
  212.3 1.3 copy-start.12
Sparse Core Ops, SparseCore 0:
  9.7 45.8 all-gather.2
  64.2 50.4 all-gather.4
  117.1 39.6 reduce-scatter.1
